TPU v7x, 128 devices: a whole 4x4x4 slice. The times are simulated.
128 devices in a mesh: row: 8 (over x, z_lo), col: 16 (over y, z_hi, core).
Axes of the slice: x: 4, y: 4, z: 4 (z_hi: 2, z_lo: 2; z = z_hi * 2 + z_lo), core: 2. Of those that a mesh axis runs over, the one named last changes fastest.
Arguments:
- left_factors: bfloat16 [32, 2688, 256], P('row', 'col'), may hold values from -0.59765625 to 0.59765625
- right_factors: bfloat16 [32, 2688, 256], P('row', 'col'), may hold values from -0.5 to 0.5
- ranks: int32 [32], replicated, may hold values from 16 to 256, as said below
Outputs:
- offdiag_update: bfloat16 [32, 32, 2688, 256], P('row', 'col')
- diag_update: bfloat16 [32, 2688, 2688], P('row', 'col')
Inputs may be any that keep to these rules, and one draw needn't show every extreme that they name: `ranks`: A tile whose number rnum(p) is 16 or more has rank at most 128, and one such tile has rank exactly 128; some tile of a smaller number has rank 256.
All inputs are finite; a program needn't handle non-finite values.
Results may differ from a plain program's by a relative error of at most 0.0055.
Values may be sent and summed in bfloat16 or wider, within the bound.
No kernel may reach another device: no remote copies, remote signals or barrier semaphores. Data moves between devices by JAX's collectives and lax.ppermute only.
A program may use at most 128 MiB of HBM per device.

v0:
```python
import jax
import jax.numpy as jnp
from jax import lax
from jax.sharding import PartitionSpec as P


def broadcast(block, axis, holder):
    block = jnp.where(lax.axis_index(axis) == holder, block, jnp.zeros_like(block))
    return lax.psum(block, axis)


def per_device(left_factors, right_factors, ranks):
    n_row = lax.axis_size("row")
    n_col = lax.axis_size("col")
    my_row = lax.axis_index("row")
    my_col = lax.axis_index("col")
    tile_rows = left_factors.shape[0]
    total = tile_rows * n_row
    tile_cols = total // n_col
    width = right_factors.shape[2]
    my_ranks = lax.dynamic_slice_in_dim(ranks, my_row * tile_rows, tile_rows, 0)
    keeper = (jnp.arange(width, dtype=jnp.int32)[None, :] < my_ranks[:, None]).astype(jnp.bfloat16)
    masked = right_factors * keeper[:, None, :]
    row_num = jnp.arange(tile_rows, dtype=jnp.int32) * n_row + my_row
    col_num = jnp.arange(tile_cols, dtype=jnp.int32) * n_col + my_col
    left_full, right_full = (
        lax.all_gather(left_factors, "col", axis=1, tiled=True),
        lax.all_gather(masked, "col", axis=1, tiled=True),
    )
    local_spot = col_num // n_row
    chosen = jnp.take(right_full, local_spot, axis=0)
    col_right = broadcast(chosen, "row", my_col % n_row)
    pair = jnp.einsum("pnk,qnl->pqkl", right_full, col_right, preferred_element_type=jnp.float32)
    selfpair = jnp.einsum(
        "pnk,pnl->pkl", right_full, right_full, preferred_element_type=jnp.float32
    )
    pair_low = pair.astype(jnp.bfloat16)
    update = jnp.einsum("pnk,pqkl->pqnl", left_full, pair_low, preferred_element_type=jnp.float32)
    lower = row_num[:, None] > col_num[None, :]
    offdiag_update = jnp.where(lower[:, :, None, None], update, 0.0).astype(jnp.bfloat16)
    self_low = selfpair.astype(jnp.bfloat16)
    inner = jnp.einsum(
        "pnk,pkl->pnl", left_factors, self_low, preferred_element_type=jnp.float32
    ).astype(jnp.bfloat16)
    diag_update = jnp.einsum(
        "pnl,pml->pnm", inner, left_full, preferred_element_type=jnp.float32
    ).astype(jnp.bfloat16)
    return (offdiag_update, diag_update)


def solution(mesh):
    in_specs = (P("row", "col", None), P("row", "col", None), P())
    out_specs = (P("row", "col", None, None), P("row", "col", None))
    return jax.shard_map(
        per_device, mesh=mesh, in_specs=in_specs, out_specs=out_specs, check_vma=False
    )
```

profile of v0, /device:TPU:1, one launch (start us, length us, event | category | flops | bytes accessed | tf_op | source)
XLA Modules:
  0.0 301.6 jit_solution(3190531290011785644)
XLA Ops:
  7.2 0.0 all-gather.3.cloned.1.call-start
  7.2 0.7 dynamic_slice.3
  7.9 0.1 fusion.19
  8.0 1.7 broadcast_multiply_fusion
  9.8 0.0 all-gather.3.cloned.1.call-update
  9.8 0.0 all-gather.5.cloned.1.call-start
  9.8 0.7 all-gather.5.cloned.1.call-update
  10.5 0.0 all-reduce.2.cloned.1.call-start
  10.7 64.8 %all-gather.3.cloned.1.call-done = bf16[4,2688,256]{2,1,0:T(8,128)(2,1)} async-done(((bf16[4,168,256]{2,1,0:T(8,128)(2,1)}), bf16[4,2688,256]{2,1,0:T(8,128)(2,1)}) %all-gather.3.cloned.1.call-update) | async-done | bytes 5505040 | tf_op jit(solution)/shard_map/all_gather | solution.py:28
  75.5 3.3 %gather_fusion = bf16[2,2688,256]{2,1,0:T(8,128)(2,1)S(1)} fusion(bf16[4,2688,256]{2,1,0:T(8,128)(2,1)} %all-gather.3.cloned.1.call-done, s32[1024]{0:T(1024)S(1)} %pad_clamp_fusion), kind=kCustom, calls=%fused_computation | custom fusion | bytes 5505032 | tf_op jit(solution)/shard_map/jit(_take)/gather | solution.py:31
  78.8 1.9 select_select_fusion
  80.7 0.0 all-reduce.2.cloned.1.call-update
  80.7 0.1 broadcast_compare_fusion
  80.8 0.0 copy-start
  80.8 6.3 %convolution_convert_fusion.1 = bf16[4,256,256]{2,1,0:T(8,128)(2,1)S(1)} fusion(bf16[4,2688,256]{2,1,0:T(8,128)(2,1)} %all-gather.3.cloned.1.call-done), kind=kOutput, calls=%fused_computation.11 | convolution fusion | flops 1409548288 | bytes 6029312 | tf_op jit(solution)/shard_map/pnk,pnl->pkl/dot_general | solution.py:34
  87.1 50.3 %all-gather.5.cloned.1.call-done = bf16[4,2688,256]{2,1,0:T(8,128)(2,1)} async-done(((bf16[4,168,256]{2,1,0:T(8,128)(2,1)}), bf16[4,2688,256]{2,1,0:T(8,128)(2,1)}) %all-gather.5.cloned.1.call-update) | async-done | bytes 5505040 | tf_op jit(solution)/shard_map/all_gather | solution.py:27
  137.4 0.0 copy-done
  137.4 6.3 %convolution_convert_fusion = bf16[4,168,2688]{2,1,0:T(8,128)(2,1)} fusion(bf16[4,2688,256]{2,1,0:T(8,128)(2,1)} %all-gather.5.cloned.1.call-done, bf16[4,256,256]{2,1,0:T(8,128)(2,1)S(1)} %convolution_convert_fusion.1, bf16[4,168,256]{2,1,0:T(8,128)(2,1)S(1)} %copy-done), kind=kOutput, calls=%fused_computation.6 | convolution fusion | flops 1014902784 | bytes 9986048 | tf_op jit(solution)/shard_map/pnl,pml->pnm/dot_general | solution.py:45
  143.7 123.5 %all-reduce.2.cloned.1.call-done = bf16[2,2688,256]{2,1,0:T(8,128)(2,1)} async-done(((bf16[2,2688,256]{2,1,0:T(8,128)(2,1)}), bf16[2,2688,256]{2,1,0:T(8,128)(2,1)}) %all-reduce.2.cloned.1.call-update) | async-done | bytes 2752528 | tf_op jit(solution)/shard_map/psum | solution.py:9
  267.2 13.3 %fusion = bf16[4,2,2688,256]{2,3,1,0:T(8,128)(2,1)} fusion(pred[4,2]{1,0:T(4,128)(4,1)S(1)} %broadcast_compare_fusion, bf16[4,2688,256]{2,1,0:T(8,128)(2,1)} %all-gather.5.cloned.1.call-done, bf16[4,2688,256]{2,1,0:T(8,128)(2,1)} %all-gather.3.cloned.1.call-done, bf16[2,2688,256]{2,1,0:T(8,128)(2,1)} %all-reduce.2.cloned.1.call-done), kind=kOutput, calls=%fused_computation.2 | convolution fusion | flops 5648678912 | bytes 24772616 | tf_op jit(solution)/shard_map/pnk,pqkl->pqnl/dot_general | solution.py:38
  280.5 14.6 %copy.5 = bf16[4,2,2688,256]{3,2,1,0:T(8,128)(2,1)} copy(bf16[4,2,2688,256]{2,3,1,0:T(8,128)(2,1)} %fusion) | data formatting | bytes 22020096
  (5 shorter events, 0.0 us)
Async XLA Ops:
  7.2 68.3 %all-gather.3.cloned.1.call-start = ((), (), s32[]{:S(2)}) async-start(), calls=%async_computation | async-start | bytes 5849088 | tf_op jit(solution)/shard_map/all_gather | solution.py:28
  9.8 127.6 %all-gather.5.cloned.1.call-start = ((), (), s32[]{:S(2)}) async-start(), calls=%async_computation.2 | async-start | bytes 5849088 | tf_op jit(solution)/shard_map/all_gather | solution.py:27
  10.5 256.7 %all-reduce.2.cloned.1.call-start = ((), (), s32[]{:S(2)}) async-start(), calls=%async_computation.1 | async-start | bytes 5505024 | tf_op jit(solution)/shard_map/psum | solution.py:9
  80.8 56.6 %copy-start = (bf16[4,168,256]{2,1,0:T(8,128)(2,1)S(1)}, bf16[4,168,256]{2,1,0:T(8,128)(2,1)}, u32[]{:S(2)}) copy-start(bf16[4,168,256]{2,1,0:T(8,128)(2,1)} %param.3) | copy-start | bytes 1032196
Sparse Core Ops, SparseCore 0:
  10.9 64.4 all-gather.2
  77.9 59.4 all-gather.4
  140.5 126.6 all-reduce.1
where the time goes:
time: 302 us
  waiting for transfers between devices  239 us (79%)
  matrix products  25.9 us (9%)
  local copies, waits for them, and re-layouts  18.6 us (6%)
  between operations  13.8 us (5%)
  other arithmetic  3.83 us (1%)
    psum x1, waiting for transfers between devices, broadcast(): return lax.psum(block, axis)  123 us
    all_gather x1, waiting for transfers between devices, per_device(): lax.all_gather(masked, 'col', axis=1, tiled=True)  64.8 us
    all_gather x1, waiting for transfers between devices, per_device(): lax.all_gather(left_factors, 'col', axis=1, tiled=True)  50.3 us
    unnamed x3, local copies, waits for them, and re-layouts  14.6 us
    dot_general x1, matrix products, per_device(): jnp.einsum('pnk,pqkl->pqnl', left_full, pair_low, preferred_element_type=...  13.3 us
    dot_general x1, matrix products, per_device(): jnp.einsum('pnl,pml->pnm', inner, left_full, preferred_element_type=jnp.f...  6.32 us
    dot_general x1, matrix products, per_device(): jnp.einsum('pnk,pnl->pkl', right_full, right_full, preferred_element_type...  6.27 us
  transfers between devices with their start and end apart: 3, of which 3 were waited for; matrix products, arithmetic and copies ran while one was open for 6% of the time, Pallas kernels for 0%

commit v1 on v0

v1 whole, which is shorter than its diff:
```python
import itertools

import jax
import jax.numpy as jnp
from jax import lax
from jax.experimental import pallas as pl
from jax.experimental.pallas import tpu as pltpu
from jax.sharding import PartitionSpec as P

AXES = ("row", "col")
BF, F32 = jnp.bfloat16, jnp.float32
PTS, CHIP, NB, LIMIT = 168, 336, 2688, 24 * 1024 * 1024


def place(x, zl, y, zh, core):
    return ((x % 4) * 2 + zl) * 16 + (y % 4) * 4 + zh * 2 + core


def mover(rule):
    ranges = (range(4), range(2), range(4), range(2), range(2))
    pairs = [(place(*d), place(*rule(*d))) for d in itertools.product(*ranges)]
    return lambda block: lax.ppermute(block, AXES, pairs)


y_split = mover(lambda x, zl, y, zh, c: (x, zl, y + 1 - 2 * c, zh, c))
z_half = mover(lambda x, zl, y, zh, c: (x, zl, y, 1 - zh, c))
core_swap = mover(lambda x, zl, y, zh, c: (x, zl, y, zh, 1 - c))
x_up = mover(lambda x, zl, y, zh, c: (x + 1, zl, y, zh, c))
x_down = mover(lambda x, zl, y, zh, c: (x - 1, zl, y, zh, c))
x_split = mover(lambda x, zl, y, zh, c: (x + 1 - 2 * c, zl, y, zh, c))


last_hop = mover(lambda x, zl, y, zh, c: (x, zl, y, 1 - zh, c) if c else (x, zl, y + 2, zh, c))


def to_column(flip):
    def rule(x, zl, y, zh, c):
        return x + y + 2 * c + flip, c, x // 2 + 2 * (zh ^ flip), x % 2, zl

    return mover(rule)


to_column_0, to_column_1 = to_column(0), to_column(1)


def pack_kernel(right_ref, left_ref, out, sem):
    copies = []
    for s, tiles in enumerate((right_ref, left_ref)):
        moves = [(tiles.at[n], out.at[3 * s + n]) for n in range(2)]
        for n in range(2):
            cut = pl.ds(128 * n, 128)
            moves.append((tiles.at[2 + n, :, pl.ds(0, 128)], out.at[3 * s + 2, :, cut]))
        copies += [pltpu.make_async_copy(*move, sem.at[4 * s + n]) for n, move in enumerate(moves)]
    for copy in copies:
        copy.start()
    for copy in copies:
        copy.wait()


def after(block, *others):
    return lax.optimization_barrier((block,) + others)[0]


def dot(a, b, ca, cb):
    return lax.dot_general(a, b, (((ca,), (cb,)), ((), ())), preferred_element_type=F32)


STEP = 672
BLOCKS = ((0, 0), (1, 0), (2, 0), (3, 0), (2, 1), (3, 1))


def block_rows(j):
    return pl.ds(pl.multiple_of(j * CHIP, 16), CHIP)


def within(values, rows, cols):
    k = lax.broadcasted_iota(jnp.int32, values.shape, 0)
    l = lax.broadcasted_iota(jnp.int32, values.shape, 1)
    return jnp.where((k < rows) & (l < cols), values, 0.0).astype(BF)


def where_am_i():
    row, col = lax.axis_index("row"), lax.axis_index("col")
    return row, col, row // 2, row % 2, col // 4, (col // 2) % 2, col % 2


def slot(y, zh, dy, dz):
    return (y + dy + 4) % 4 * 2 + (zh + dz) % 2


def column_slots(dx):
    _, _, x, zl, y, zh, core = where_am_i()
    turned = x + dx - (y % 2) * 2 - zh + 16
    return [(turned - 2 * zl - o) % 4 * 2 + (y // 2 + o) % 2 for o in range(2)]


def partial_kernel(*refs):
    chip, near, near_2, mine, theirs, cols = *refs[:3], refs[3:6], refs[6:8], refs[8:11]
    self_out, pair_out, v_out, col_out, v_buf, col_buf, vsem, csem, osem = refs[11:]
    theirs = (theirs[0], near_2.at[pl.ds(6, 3)], theirs[1])
    _, _, x, zl, y, zh, core = where_am_i()
    turn = 1 - 2 * core

    def piece(src, dy, dz, n):
        rows = block_rows(slot(y, zh, dy, dz))
        return pltpu.make_async_copy(src, v_buf.at[:, rows], vsem.at[n])

    for n, (src, dy) in enumerate(((chip, 0), (near, -turn), (near_2, turn))):
        piece(src.at[pl.ds(0, 3)], dy, 0, n).start()
    for c in range(2):
        @pl.when(core == c)
        def _():
            far_e, across, _ = mine if c == 0 else theirs
            f = theirs[2] if c == 0 else mine[2]
            sources = (across, far_e.at[0], far_e.at[1], f)
            for n, (src, at) in enumerate(zip(sources, ((0, 1), (2, 0), (-1, 1), (1, 1)))):
                piece(src, *at, 3 + n).start()
    copies = []
    for i, dx in enumerate((0, -1, 1)):
        for o, j in enumerate(column_slots(dx)):
            rows = block_rows(j)
            copies.append(
                pltpu.make_async_copy(cols[i].at[o], col_buf.at[rows], csem.at[2 * i + o])
            )
    for copy in copies:
        copy.start()
    for j in column_slots(2):
        col_buf[block_rows(j), :] = jnp.zeros((CHIP, 384), BF)
    last = block_rows(slot(y, zh, 2, 1))
    for s in range(3):
        v_buf[s, last, :] = jnp.zeros((CHIP, 256), BF)
    for n in range(7):
        piece(chip.at[pl.ds(0, 3)], 0, 0, n).wait()
    for copy in copies:
        copy.wait()
    outs = [
        pltpu.make_async_copy(v_buf, v_out, osem.at[0]),
        pltpu.make_async_copy(col_buf, col_out, osem.at[1]),
    ]
    for copy in outs:
        copy.start()
    turned = col_buf[...].T
    for s in range(3):
        size = 256 if s < 2 else 384
        pair_out[:size, s * 256 : (s + 1) * 256] = dot(turned[:size], v_buf[s], 1, 0)
        self_out[s] = dot(v_buf[s], v_buf[s], 0, 0)
    for copy in outs:
        copy.wait()


def final_kernel(rank_ref, *refs):
    chip, near, near_2, left_ref, self_ref, pair_ref, v_in, col_in, last_col = refs[:9]
    mine, theirs = refs[9:13], refs[13:16]
    theirs = (theirs[0], near_2.at[pl.ds(6, 3)], *theirs[1:])
    off, diag = refs[16:18]
    v_buf, u_buf, col_buf, zero, stage, wide, vsem, usem, csem, zsem, osem, dsem = refs[18:]
    row, col, x, zl, y, zh, core = where_am_i()
    turn = 1 - 2 * core

    def piece(src, dy, dz, n):
        rows = block_rows(slot(y, zh, dy, dz))
        return pltpu.make_async_copy(src, u_buf.at[:, rows], usem.at[n])

    at_last = slot(y, zh, 2, 1)
    at_cols = column_slots(2)

    def v_copy(src, n):
        return pltpu.make_async_copy(src, v_buf.at[n], vsem.at[n])

    def col_copy(src, n):
        return pltpu.make_async_copy(src, col_buf.at[n], csem.at[n])

    for n in range(2):
        v_copy(v_in.at[:, block_rows(at_cols[n])], n).start()
        col_copy(last_col.at[n], n).start()

        @pl.when(at_cols[n] == at_last)
        def _():
            col_copy(last_col.at[n], 2).start()

    @pl.when((at_cols[0] != at_last) & (at_cols[1] != at_last))
    def _():
        col_copy(col_in.at[block_rows(at_last)], 2).start()

    for n, (src, dy) in enumerate(((chip, 0), (near, -turn), (near_2, turn))):
        piece(src.at[pl.ds(3, 3)], dy, 0, n).start()
    for c in range(2):
        @pl.when(core == c)
        def _():
            v_copy((mine if c == 0 else theirs)[3], 2).start()
            far_e, across, _, g = theirs if c == 0 else mine
            f = mine[2] if c == 0 else theirs[2]
            sources = (across, far_e.at[0], far_e.at[1], f, g)
            for n, (src, at) in enumerate(zip(sources, ((0, 1), (2, 0), (1, 1), (-1, 1), (2, 1)))):
                piece(src, *at, 3 + n).start()

    zero[...] = jnp.zeros_like(zero)
    zeros = [pltpu.make_async_copy(zero, off.at[p, 1], zsem.at[p]) for p in range(2)]
    for copy in zeros:
        copy.start()
    for i in range(2):
        for n in (4, 5):
            stage[i, n, :, 128:] = jnp.zeros((STEP, 128), BF)
    row_ranks = [rank_ref[row * 4 + p] for p in range(4)]
    col_ranks = [rank_ref[col % 8 * 4 + 2 * q + col // 8] for q in range(2)]

    def kept(p, q):
        return jnp.where(p * 8 + row > q * 16 + col, row_ranks[p], 0)

    for n in range(3):
        v_copy(v_in.at[:, pl.ds(0, CHIP)], n).wait()
        col_copy(last_col.at[0], n).wait()
    turned = [col_buf[n].T for n in range(3)]

    def whole_pair(s, rows):
        total = pair_ref[:rows, s * 256 : (s + 1) * 256] + dot(turned[2][:rows], v_buf[2, s], 1, 0)
        for n in range(2):
            more = dot(turned[n][:rows], v_buf[n, s], 1, 0)
            total += jnp.where(at_cols[n] != at_last, more, 0.0)
        return total.T

    ready = [[within(whole_pair(p, 256), kept(p, 0), col_ranks[0])] for p in range(2)]
    both = whole_pair(2, 384)
    for p in range(2, 4):
        rows = slice((p - 2) * 128, (p - 1) * 128)
        cuts = (slice(0, 256), slice(256, 384))
        ready.append(
            [within(both[rows, cut], kept(p, q), col_ranks[q]) for q, cut in enumerate(cuts)]
        )
    for n in range(8):
        piece(chip.at[pl.ds(3, 3)], 0, 0, n).wait()

    def sends(i):
        rows = slice(i * STEP, (i + 1) * STEP)
        return [
            pltpu.make_async_copy(stage.at[i % 2, n], off.at[p, q, rows], osem.at[i % 2, n])
            for n, (p, q) in enumerate(BLOCKS)
        ]

    steps = NB // STEP
    for i in range(steps):
        if i >= 2:
            for copy in sends(i - 2):
                copy.wait()
        rows = slice(i * STEP, (i + 1) * STEP)
        for p in range(2):
            stage[i % 2, p] = dot(u_buf[p, rows], ready[p][0], 1, 0).astype(BF)
        for p in range(2, 4):
            part = u_buf[2, rows, (p - 2) * 128 : (p - 1) * 128]
            stage[i % 2, p] = dot(part, ready[p][0], 1, 0).astype(BF)
            stage[i % 2, p + 2, :, :128] = dot(part, ready[p][1], 1, 0).astype(BF)
        for copy in sends(i):
            copy.start()

    diag_copies = []
    for p in range(4):
        s = min(p, 2)
        cut = slice(0, 256) if p < 2 else slice((p - 2) * 128, (p - 1) * 128)
        if p < 3:
            own = self_ref[s] + dot(v_buf[2, s], v_buf[2, s], 0, 0)
        square = within(own[cut, cut], row_ranks[p], row_ranks[p])
        inner = dot(left_ref[3 + s, :, cut], square, 1, 0).astype(BF)
        wide[p] = dot(inner, u_buf[s, :, cut], 1, 1).astype(BF)
        diag_copies.append(pltpu.make_async_copy(wide.at[p], diag.at[p], dsem.at[p]))
        diag_copies[-1].start()
    for i in range(steps - 2, steps):
        for copy in sends(i):
            copy.wait()
    for copy in zeros + diag_copies:
        copy.wait()


SMEM = pl.BlockSpec(memory_space=pltpu.SMEM)
VMEM = pl.BlockSpec(memory_space=pltpu.VMEM)
ANY = pl.BlockSpec(memory_space=pl.ANY)


def per_device(left_factors, right_factors, ranks):
    col = lax.axis_index("col")
    zh, core = (col // 2) % 2, col % 2
    first = core == 0
    shape, params = jax.ShapeDtypeStruct, pltpu.CompilerParams(vmem_limit_bytes=LIMIT)
    dma = pltpu.SemaphoreType.DMA
    own = pl.pallas_call(
        pack_kernel,
        out_shape=shape((6, PTS, 256), BF),
        in_specs=[ANY] * 2,
        out_specs=VMEM,
        scratch_shapes=[dma((8,))],
        compiler_params=params,
    )(right_factors, left_factors)
    other = core_swap(own)
    chip = jnp.concatenate([jnp.where(first, own, other), jnp.where(first, other, own)], axis=1)

    def column_block(a):
        near = jnp.where(a == 0, chip[0], chip[1])
        far = jnp.where(a == 0, chip[2, :, :128], chip[2, :, 128:])
        return jnp.concatenate([near, far], axis=1)

    role = jnp.where(first, chip[:3], chip[3:])
    chip, role, block0, block1 = lax.optimization_barrier(
        (chip, role, column_block(zh), column_block(1 - zh))
    )
    near, across = y_split(chip), z_half(role)
    got = jnp.stack([to_column_0(block0), to_column_1(block1)])
    near, across, got = lax.optimization_barrier((near, across, got))
    far_e = y_split(jnp.stack([jnp.where(first, near[:3], near[3:]), across]))
    f = z_half(jnp.where(first, near[3:], near[:3]))
    near_2 = core_swap(jnp.concatenate([near, across]))
    left_col, right_col = x_up(got), x_down(got)
    far_e, f, left_col, right_col = lax.optimization_barrier((far_e, f, left_col, right_col))
    g = last_hop(jnp.where(first, across, far_e[0]))
    last_col = x_split(jnp.where(first, left_col, right_col))
    far_e2, f_2 = core_swap(far_e), core_swap(f)
    selfpart, pairpart, v_full, col_full = pl.pallas_call(
        partial_kernel,
        out_shape=(
            shape((3, 256, 256), F32), shape((384, 768), F32),
            shape((3, NB, 256), BF), shape((NB, 384), BF),
        ),
        in_specs=[ANY] * 11,
        out_specs=(VMEM, VMEM, ANY, ANY),
        scratch_shapes=[
            pltpu.VMEM((3, NB, 256), BF), pltpu.VMEM((NB, 384), BF), dma((7,)), dma((6,)), dma((2,)),
        ],
        compiler_params=params,
        cost_estimate=pl.CostEstimate(
            flops=4_000_000_000, bytes_accessed=15_000_000, transcendentals=0
        ),
    )(chip, near, near_2, far_e, across, f, far_e2, f_2, got, left_col, right_col)
    g_2 = core_swap(after(g, selfpart))
    return pl.pallas_call(
        final_kernel,
        out_shape=(shape((4, 2, NB, 256), BF), shape((4, PTS, NB), BF)),
        in_specs=[SMEM] + [ANY] * 3 + [VMEM] * 3 + [ANY] * 10,
        out_specs=(ANY, ANY),
        scratch_shapes=[
            pltpu.VMEM((3, 3, CHIP, 256), BF),
            pltpu.VMEM((3, NB, 256), BF),
            pltpu.VMEM((3, CHIP, 384), BF),
            pltpu.VMEM((NB, 256), BF),
            pltpu.VMEM((2, 6, STEP, 256), BF),
            pltpu.VMEM((4, PTS, NB), BF),
            dma((3,)), dma((8,)), dma((3,)), dma((2,)), dma((2, 6)), dma((4,)),
        ],
        compiler_params=params,
        cost_estimate=pl.CostEstimate(
            flops=6_000_000_000, bytes_accessed=25_000_000, transcendentals=0
        ),
    )(
        ranks, chip, near, near_2, own, selfpart, pairpart, v_full, col_full, last_col,
        far_e, across, f, g, far_e2, f_2, g_2,
    )


def solution(mesh):
    in_specs = (P("row", "col", None), P("row", "col", None), P())
    out_specs = (P("row", "col", None, None), P("row", "col", None))
    return jax.shard_map(
        per_device, mesh=mesh, in_specs=in_specs, out_specs=out_specs, check_vma=False
    )
```

time: 302 us -> 77.2 us (0.26)
  waiting for transfers between devices: 239 us -> 26.5 us
  starting transfers between devices: 0.12 us -> 27.1 us
  matrix products: 25.9 us -> 0 us
  Pallas kernels: 0 us -> 19.6 us
  local copies, waits for them, and re-layouts: 18.6 us -> 1.96 us
  between operations: 13.8 us -> 0.97 us
    psum x1 -> x0, waiting for transfers between devices: 123 us -> none  [broadcast(): return lax.psum(block, axis)]
    all_gather x2 -> x0, waiting for transfers between devices: 115 us -> none  [the longest x1 64.8 us: per_device(): lax.all_gather(masked, 'col', axis=1, tiled=True)]
    ppermute x0 -> x15, starting transfers between devices: none -> 27.1 us  [mover(): return lambda block: lax.ppermute(block, AXES, pairs)]
    ppermute x0 -> x15, waiting for transfers between devices: none -> 26.5 us  [mover(): return lambda block: lax.ppermute(block, AXES, pairs)]
    dot_general x3 -> x0, matrix products: 25.9 us -> none  [the longest x1 13.3 us: per_device(): jnp.einsum('pnk,pqkl->pqnl', left_full, pair_low, preferred_element_type=...]
    pallas_call x0 -> x3, Pallas kernels: none -> 19.6 us  [the longest x1 11.8 us: per_device(): pl.pallas_call(final_kernel, out_shape=(shape((4, 2, NB, 256), BF), shape...]
    unnamed x3 -> x6, local copies, waits for them, and re-layouts: 14.6 us -> 1.96 us
    gather x1 -> x0, local copies, waits for them, and re-layouts: 3.28 us -> none  [per_device(): chosen = jnp.take(right_full, local_spot, axis=0)]
  transfers between devices with their start and end apart: 3 -> 15, of which waited for: 3 -> 6; matrix products, arithmetic and copies ran while one was open for 6% -> 0% of each run, Pallas kernels for 0% -> 9%
where the time goes in v1:
time: 77.2 us; the launch traced here: 77 us
  starting transfers between devices  27.1 us (35%)
  waiting for transfers between devices  26.5 us (34%)
  Pallas kernels  19.6 us (25%)
  local copies, waits for them, and re-layouts  1.96 us (3%)
  between operations  0.97 us (1%)
  other arithmetic  0.95 us (1%)
    ppermute x15, starting transfers between devices, mover(): return lambda block: lax.ppermute(block, AXES, pairs)  27.1 us
    ppermute x15, waiting for transfers between devices, mover(): return lambda block: lax.ppermute(block, AXES, pairs)  26.5 us
    pallas_call x1, Pallas kernels, per_device(): pl.pallas_call(final_kernel, out_shape=(shape((4, 2, NB, 256), BF), shape...  11.8 us
    pallas_call x1, Pallas kernels, per_device(): pl.pallas_call(partial_kernel, out_shape=(shape((3, 256, 256), F32), shap...  7.24 us
    unnamed x6, local copies, waits for them, and re-layouts  1.96 us
  transfers between devices with their start and end apart: 15, of which 6 were waited for; matrix products, arithmetic and copies ran while one was open for 0% of the time, Pallas kernels for 9%

profile of v1, /device:TPU:1, one launch (start us, length us, event | category | flops | bytes accessed | tf_op | source)
XLA Modules:
  0.0 77.0 jit_solution(14153962949729776566)
XLA Ops:
  0.6 1.0 %copy-done = bf16[4,168,256]{2,1,0:T(8,128)(2,1)S(1)} copy-done((bf16[4,168,256]{2,1,0:T(8,128)(2,1)S(1)}, bf16[4,168,256]{2,1,0:T(8,128)(2,1)}, u32[]{:S(2)}) %copy-start) | copy-done | bytes 344088
  1.6 1.0 %copy-done.1 = bf16[4,168,256]{2,1,0:T(8,128)(2,1)S(1)} copy-done((bf16[4,168,256]{2,1,0:T(8,128)(2,1)S(1)}, bf16[4,168,256]{2,1,0:T(8,128)(2,1)}, u32[]{:S(2)}) %copy-start.1) | copy-done | bytes 344088
  2.6 0.5 shard_map.50.refs_3_
  3.1 1.5 %collective-permute-start = (bf16[6,168,256]{2,1,0:T(8,128)(2,1)S(1)}, bf16[6,168,256]{2,1,0:T(8,128)(2,1)S(1)}, u32[]{:S(2)}, u32[]{:S(2)}) collective-permute-start(bf16[6,168,256]{2,1,0:T(8,128)(2,1)S(1)} %shard_map.50.refs_3_), channel_id=1, source_target_pairs={{0,1},{1,0},{2,3},{3,2},{4,5},{5,4},{6,7},{7,6},{8,9},{9,8},{10,11... | collective-permute-start | bytes 1548296 | tf_op jit(solution)/shard_map/ppermute | solution.py:22
  4.6 1.5 %collective-permute-done = bf16[6,168,256]{2,1,0:T(8,128)(2,1)S(1)} collective-permute-done((bf16[6,168,256]{2,1,0:T(8,128)(2,1)S(1)}, bf16[6,168,256]{2,1,0:T(8,128)(2,1)S(1)}, u32[]{:S(2)}, u32[]{:S(2)}) %collective-permute-start) | collective-permute-done | bytes 516128 | tf_op jit(solution)/shard_map/ppermute | solution.py:22
  6.2 0.1 fusion.1
  6.6 2.9 %collective-permute-start.1 = (bf16[6,336,256]{2,1,0:T(8,128)(2,1)S(1)}, bf16[6,336,256]{2,1,0:T(8,128)(2,1)S(1)}, u32[]{:S(2)}, u32[]{:S(2)}) collective-permute-start(bf16[6,336,256]{2,1,0:T(8,128)(2,1)S(1)} %pad_maximum_fusion.refs_0_), channel_id=1, source_target_pairs={{0,4},{1,13},{2,6},{3,15},{4,8},{5,1},{6,10},{7,3},{8,12},{9,5},{1... | collective-permute-start | bytes 3096584 | tf_op jit(solution)/shard_map/ppermute | solution.py:22
  9.5 3.6 %collective-permute-start.2 = (bf16[3,336,256]{2,1,0:T(8,128)(2,1)S(1)}, bf16[3,336,256]{2,1,0:T(8,128)(2,1)S(1)}, u32[]{:S(2)}, u32[]{:S(2)}) collective-permute-start(bf16[3,336,256]{2,1,0:T(8,128)(2,1)S(1)} %fusion.1), channel_id=1, source_target_pairs={{0,2},{1,3},{2,0},{3,1},{4,6},{5,7},{6,4},{7,5},{8,10},{9,11},{10,... | collective-permute-start | bytes 1548296 | tf_op jit(solution)/shard_map/ppermute | solution.py:22
  13.1 4.5 %collective-permute-start.3 = (bf16[336,384]{1,0:T(8,128)(2,1)S(1)}, bf16[336,384]{1,0:T(8,128)(2,1)S(1)}, u32[]{:S(2)}, u32[]{:S(2)}) collective-permute-start(bf16[336,384]{1,0:T(8,128)(2,1)S(1)} %get-tuple-element.20), channel_id=1, source_target_pairs={{0,0},{1,80},{2,8},{3,88},{4,32},{5,112},{6,40},{7,120},{8,64},{9,... | collective-permute-start | bytes 774152 | tf_op jit(solution)/shard_map/ppermute | solution.py:22
  17.6 4.0 %collective-permute-start.4 = (bf16[336,384]{1,0:T(8,128)(2,1)S(1)}, bf16[336,384]{1,0:T(8,128)(2,1)S(1)}, u32[]{:S(2)}, u32[]{:S(2)}) collective-permute-start(bf16[336,384]{1,0:T(8,128)(2,1)S(1)} %get-tuple-element.21), channel_id=1, source_target_pairs={{0,40},{1,120},{2,32},{3,112},{4,72},{5,24},{6,64},{7,16},{8,104},... | collective-permute-start | bytes 774152 | tf_op jit(solution)/shard_map/ppermute | solution.py:22
  21.6 12.2 %collective-permute-done.3 = bf16[336,384]{1,0:T(8,128)(2,1)S(1)} collective-permute-done((bf16[336,384]{1,0:T(8,128)(2,1)S(1)}, bf16[336,384]{1,0:T(8,128)(2,1)S(1)}, u32[]{:S(2)}, u32[]{:S(2)}) %collective-permute-start.3) | collective-permute-done | bytes 258080 | tf_op jit(solution)/shard_map/ppermute | solution.py:22
  34.1 1.5 %collective-permute-start.9 = (bf16[2,336,384]{2,1,0:T(8,128)(2,1)S(1)}, bf16[2,336,384]{2,1,0:T(8,128)(2,1)S(1)}, u32[]{:S(2)}, u32[]{:S(2)}) collective-permute-start(bf16[2,336,384]{2,1,0:T(8,128)(2,1)S(1)} %pad_maximum_fusion.3.refs_8_), channel_id=1, source_target_pairs={{0,96},{1,97},{2,98},{3,99},{4,100},{5,101},{6,102},{7,103},{8,104... | collective-permute-start | bytes 1548296 | tf_op jit(solution)/shard_map/ppermute | solution.py:22
  35.7 1.4 %collective-permute-start.7 = (bf16[3,336,256]{2,1,0:T(8,128)(2,1)S(1)}, bf16[3,336,256]{2,1,0:T(8,128)(2,1)S(1)}, u32[]{:S(2)}, u32[]{:S(2)}) collective-permute-start(bf16[3,336,256]{2,1,0:T(8,128)(2,1)S(1)} %get-tuple-element.37), channel_id=1, source_target_pairs={{0,2},{1,3},{2,0},{3,1},{4,6},{5,7},{6,4},{7,5},{8,10},{9,11},{10,... | collective-permute-start | bytes 1548296 | tf_op jit(solution)/shard_map/ppermute | solution.py:22
  37.1 0.1 pad_maximum_fusion.1
  37.2 2.1 %collective-permute-start.5 = (bf16[9,336,256]{2,1,0:T(8,128)(2,1)S(1)}, bf16[9,336,256]{2,1,0:T(8,128)(2,1)S(1)}, u32[]{:S(2)}, u32[]{:S(2)}) collective-permute-start(bf16[9,336,256]{2,1,0:T(8,128)(2,1)S(1)} %pad_maximum_fusion.1), channel_id=1, source_target_pairs={{0,1},{1,0},{2,3},{3,2},{4,5},{5,4},{6,7},{7,6},{8,9},{9,8},{10,11... | collective-permute-start | bytes 4644872 | tf_op jit(solution)/shard_map/ppermute | solution.py:22
  39.3 8.6 %collective-permute-done.9.refs_10_ = bf16[2,336,384]{2,1,0:T(8,128)(2,1)S(1)} collective-permute-done((bf16[2,336,384]{2,1,0:T(8,128)(2,1)S(1)}, bf16[2,336,384]{2,1,0:T(8,128)(2,1)S(1)}, u32[]{:S(2)}, u32[]{:S(2)}) %collective-permute-start.9) | collective-permute-done | bytes 516128 | tf_op jit(solution)/shard_map/ppermute | solution.py:22
  47.9 1.9 %collective-permute-done.8.refs_9_ = bf16[2,336,384]{2,1,0:T(8,128)(2,1)S(1)} collective-permute-done((bf16[2,336,384]{2,1,0:T(8,128)(2,1)S(1)}, bf16[2,336,384]{2,1,0:T(8,128)(2,1)S(1)}, u32[]{:S(2)}, u32[]{:S(2)}) %collective-permute-start.8) | collective-permute-done | bytes 516128 | tf_op jit(solution)/shard_map/ppermute | solution.py:22
  49.9 0.3 collective-permute-done.7.refs_5_.refs_11_
  50.2 1.2 %collective-permute-start.10 = (bf16[2,3,336,256]{3,2,1,0:T(8,128)(2,1)S(1)}, bf16[2,3,336,256]{3,2,1,0:T(8,128)(2,1)S(1)}, u32[]{:S(2)}, u32[]{:S(2)}) collective-permute-start(bf16[2,3,336,256]{3,2,1,0:T(8,128)(2,1)S(1)} %collective-permute-done.6.refs_3_.refs_9_), channel_id=1, source_target_pairs={{0,1},{1,0},{2,3},{3,2},{4,5},{5,4},{6,7},{7,6},{8,9},{9,8},{10,11... | collective-permute-start | bytes 3096584 | tf_op jit(solution)/shard_map/ppermute | solution.py:22
  51.4 1.5 %collective-permute-start.13 = (bf16[3,336,256]{2,1,0:T(8,128)(2,1)S(1)}, bf16[3,336,256]{2,1,0:T(8,128)(2,1)S(1)}, u32[]{:S(2)}, u32[]{:S(2)}) collective-permute-start(bf16[3,336,256]{2,1,0:T(8,128)(2,1)S(1)} %bitcast_select_fusion), channel_id=1, source_target_pairs={{0,8},{1,3},{2,10},{3,1},{4,12},{5,7},{6,14},{7,5},{8,0},{9,11},{1... | collective-permute-start | bytes 1548296 | tf_op jit(solution)/shard_map/ppermute | solution.py:22
  53.0 2.7 %collective-permute-start.12 = (bf16[2,336,384]{2,1,0:T(8,128)(2,1)S(1)}, bf16[2,336,384]{2,1,0:T(8,128)(2,1)S(1)}, u32[]{:S(2)}, u32[]{:S(2)}) collective-permute-start(bf16[2,336,384]{2,1,0:T(8,128)(2,1)S(1)} %broadcast_select_fusion), channel_id=1, source_target_pairs={{0,32},{1,97},{2,34},{3,99},{4,36},{5,101},{6,38},{7,103},{8,40},{... | collective-permute-start | bytes 1548296 | tf_op jit(solution)/shard_map/ppermute | solution.py:22
  55.8 7.2 %shard_map.51 = (f32[3,256,256]{2,1,0:T(8,128)S(1)}, f32[384,768]{1,0:T(8,128)S(1)}, bf16[3,2688,256]{2,1,0:T(8,128)(2,1)S(1)}, bf16[2688,384]{1,0:T(8,128)(2,1)S(1)}) custom-call(bf16[6,336,256]{2,1,0:T(8,128)(2,1)S(1)} %pad_maximum_fusion.refs_0_, bf16[6,336,256]{2,1,0:T(8,128)(2,1)S(1)} %collective-permute-done.1.refs_1_, ...), custom_call_target="tpu_custom_call" | custom-call | flops 4000000000 | bytes 15000000 | tf_op jit(solution)/shard_map/pallas_call | solution.py:315
  63.1 1.9 %collective-permute-done.14.refs_15_ = bf16[3,336,256]{2,1,0:T(8,128)(2,1)S(1)} collective-permute-done((bf16[3,336,256]{2,1,0:T(8,128)(2,1)S(1)}, bf16[3,336,256]{2,1,0:T(8,128)(2,1)S(1)}, u32[]{:S(2)}, u32[]{:S(2)}) %collective-permute-start.14) | collective-permute-done | bytes 516128 | tf_op jit(solution)/shard_map/ppermute | solution.py:22
  65.0 11.8 %shard_map.52 = (bf16[4,2,2688,256]{3,2,1,0:T(8,128)(2,1)}, bf16[4,168,2688]{2,1,0:T(8,128)(2,1)}) custom-call(s32[32]{0:T(128)S(1)} %copy-done.2, bf16[6,336,256]{2,1,0:T(8,128)(2,1)S(1)} %pad_maximum_fusion.refs_0_, bf16[6,336,256]{2,1,0:T(8,128)(2,1)S(1)} %collective-permute-done.1.refs_1_, bf16[9,336,256]{2,1,0:T(8,128)(2,1)S(1)} %collective-permute-done.5.refs_2_, ...), custom_call_target="tpu_custom_call" | custom-call | flops 6000000000 | bytes 25000000 | tf_op jit(solution)/shard_map/pallas_call | solution.py:332
  (28 shorter events, 0.9 us)
Async XLA Ops:
  0.6 1.0 %copy-start = (bf16[4,168,256]{2,1,0:T(8,128)(2,1)S(1)}, bf16[4,168,256]{2,1,0:T(8,128)(2,1)}, u32[]{:S(2)}) copy-start(bf16[4,168,256]{2,1,0:T(8,128)(2,1)} %right_ref.1) | copy-start | bytes 1032196
  1.6 1.0 %copy-start.1 = (bf16[4,168,256]{2,1,0:T(8,128)(2,1)S(1)}, bf16[4,168,256]{2,1,0:T(8,128)(2,1)}, u32[]{:S(2)}) copy-start(bf16[4,168,256]{2,1,0:T(8,128)(2,1)} %left_ref.1) | copy-start | bytes 1032196
  3.1 3.0 %collective-permute-start = (bf16[6,168,256]{2,1,0:T(8,128)(2,1)S(1)}, bf16[6,168,256]{2,1,0:T(8,128)(2,1)S(1)}, u32[]{:S(2)}, u32[]{:S(2)}) collective-permute-start(bf16[6,168,256]{2,1,0:T(8,128)(2,1)S(1)} %shard_map.50.refs_3_), channel_id=1, source_target_pairs={{0,1},{1,0},{2,3},{3,2},{4,5},{5,4},{6,7},{7,6},{8,9},{9,8},{10,11... | collective-permute-start | bytes 1548296 | tf_op jit(solution)/shard_map/ppermute | solution.py:22
  6.6 27.2 %collective-permute-start.1 = (bf16[6,336,256]{2,1,0:T(8,128)(2,1)S(1)}, bf16[6,336,256]{2,1,0:T(8,128)(2,1)S(1)}, u32[]{:S(2)}, u32[]{:S(2)}) collective-permute-start(bf16[6,336,256]{2,1,0:T(8,128)(2,1)S(1)} %pad_maximum_fusion.refs_0_), channel_id=1, source_target_pairs={{0,4},{1,13},{2,6},{3,15},{4,8},{5,1},{6,10},{7,3},{8,12},{9,5},{1... | collective-permute-start | bytes 3096584 | tf_op jit(solution)/shard_map/ppermute | solution.py:22
  9.5 24.3 %collective-permute-start.2 = (bf16[3,336,256]{2,1,0:T(8,128)(2,1)S(1)}, bf16[3,336,256]{2,1,0:T(8,128)(2,1)S(1)}, u32[]{:S(2)}, u32[]{:S(2)}) collective-permute-start(bf16[3,336,256]{2,1,0:T(8,128)(2,1)S(1)} %fusion.1), channel_id=1, source_target_pairs={{0,2},{1,3},{2,0},{3,1},{4,6},{5,7},{6,4},{7,5},{8,10},{9,11},{10,... | collective-permute-start | bytes 1548296 | tf_op jit(solution)/shard_map/ppermute | solution.py:22
  13.1 20.7 %collective-permute-start.3 = (bf16[336,384]{1,0:T(8,128)(2,1)S(1)}, bf16[336,384]{1,0:T(8,128)(2,1)S(1)}, u32[]{:S(2)}, u32[]{:S(2)}) collective-permute-start(bf16[336,384]{1,0:T(8,128)(2,1)S(1)} %get-tuple-element.20), channel_id=1, source_target_pairs={{0,0},{1,80},{2,8},{3,88},{4,32},{5,112},{6,40},{7,120},{8,64},{9,... | collective-permute-start | bytes 774152 | tf_op jit(solution)/shard_map/ppermute | solution.py:22
  17.6 16.2 %collective-permute-start.4 = (bf16[336,384]{1,0:T(8,128)(2,1)S(1)}, bf16[336,384]{1,0:T(8,128)(2,1)S(1)}, u32[]{:S(2)}, u32[]{:S(2)}) collective-permute-start(bf16[336,384]{1,0:T(8,128)(2,1)S(1)} %get-tuple-element.21), channel_id=1, source_target_pairs={{0,40},{1,120},{2,32},{3,112},{4,72},{5,24},{6,64},{7,16},{8,104},... | collective-permute-start | bytes 774152 | tf_op jit(solution)/shard_map/ppermute | solution.py:22
  34.1 16.1 %collective-permute-start.6 = (bf16[2,3,336,256]{3,2,1,0:T(8,128)(2,1)S(1)}, bf16[2,3,336,256]{3,2,1,0:T(8,128)(2,1)S(1)}, u32[]{:S(2)}, u32[]{:S(2)}) collective-permute-start(bf16[2,3,336,256]{3,2,1,0:T(8,128)(2,1)S(1)} %pad_maximum_fusion.2), channel_id=1, source_target_pairs={{0,4},{1,13},{2,6},{3,15},{4,8},{5,1},{6,10},{7,3},{8,12},{9,5},{1... | collective-permute-start | bytes 3096584 | tf_op jit(solution)/shard_map/ppermute | solution.py:22
  34.1 13.8 %collective-permute-start.9 = (bf16[2,336,384]{2,1,0:T(8,128)(2,1)S(1)}, bf16[2,336,384]{2,1,0:T(8,128)(2,1)S(1)}, u32[]{:S(2)}, u32[]{:S(2)}) collective-permute-start(bf16[2,336,384]{2,1,0:T(8,128)(2,1)S(1)} %pad_maximum_fusion.3.refs_8_), channel_id=1, source_target_pairs={{0,96},{1,97},{2,98},{3,99},{4,100},{5,101},{6,102},{7,103},{8,104... | collective-permute-start | bytes 1548296 | tf_op jit(solution)/shard_map/ppermute | solution.py:22
  35.7 14.2 %collective-permute-start.8 = (bf16[2,336,384]{2,1,0:T(8,128)(2,1)S(1)}, bf16[2,336,384]{2,1,0:T(8,128)(2,1)S(1)}, u32[]{:S(2)}, u32[]{:S(2)}) collective-permute-start(bf16[2,336,384]{2,1,0:T(8,128)(2,1)S(1)} %pad_maximum_fusion.3.refs_8_), channel_id=1, source_target_pairs={{0,32},{1,33},{2,34},{3,35},{4,36},{5,37},{6,38},{7,39},{8,40},{9,... | collective-permute-start | bytes 1548296 | tf_op jit(solution)/shard_map/ppermute | solution.py:22
  35.7 14.5 %collective-permute-start.7 = (bf16[3,336,256]{2,1,0:T(8,128)(2,1)S(1)}, bf16[3,336,256]{2,1,0:T(8,128)(2,1)S(1)}, u32[]{:S(2)}, u32[]{:S(2)}) collective-permute-start(bf16[3,336,256]{2,1,0:T(8,128)(2,1)S(1)} %get-tuple-element.37), channel_id=1, source_target_pairs={{0,2},{1,3},{2,0},{3,1},{4,6},{5,7},{6,4},{7,5},{8,10},{9,11},{10,... | collective-permute-start | bytes 1548296 | tf_op jit(solution)/shard_map/ppermute | solution.py:22
  37.2 18.5 %collective-permute-start.5 = (bf16[9,336,256]{2,1,0:T(8,128)(2,1)S(1)}, bf16[9,336,256]{2,1,0:T(8,128)(2,1)S(1)}, u32[]{:S(2)}, u32[]{:S(2)}) collective-permute-start(bf16[9,336,256]{2,1,0:T(8,128)(2,1)S(1)} %pad_maximum_fusion.1), channel_id=1, source_target_pairs={{0,1},{1,0},{2,3},{3,2},{4,5},{5,4},{6,7},{7,6},{8,9},{9,8},{10,11... | collective-permute-start | bytes 4644872 | tf_op jit(solution)/shard_map/ppermute | solution.py:22
  50.2 5.6 %collective-permute-start.10 = (bf16[2,3,336,256]{3,2,1,0:T(8,128)(2,1)S(1)}, bf16[2,3,336,256]{3,2,1,0:T(8,128)(2,1)S(1)}, u32[]{:S(2)}, u32[]{:S(2)}) collective-permute-start(bf16[2,3,336,256]{3,2,1,0:T(8,128)(2,1)S(1)} %collective-permute-done.6.refs_3_.refs_9_), channel_id=1, source_target_pairs={{0,1},{1,0},{2,3},{3,2},{4,5},{5,4},{6,7},{7,6},{8,9},{9,8},{10,11... | collective-permute-start | bytes 3096584 | tf_op jit(solution)/shard_map/ppermute | solution.py:22
  51.4 4.4 %collective-permute-start.11 = (bf16[3,336,256]{2,1,0:T(8,128)(2,1)S(1)}, bf16[3,336,256]{2,1,0:T(8,128)(2,1)S(1)}, u32[]{:S(2)}, u32[]{:S(2)}) collective-permute-start(bf16[3,336,256]{2,1,0:T(8,128)(2,1)S(1)} %collective-permute-done.7.refs_5_.refs_11_), channel_id=1, source_target_pairs={{0,1},{1,0},{2,3},{3,2},{4,5},{5,4},{6,7},{7,6},{8,9},{9,8},{10,11... | collective-permute-start | bytes 1548296 | tf_op jit(solution)/shard_map/ppermute | solution.py:22
  51.4 11.6 %collective-permute-start.13 = (bf16[3,336,256]{2,1,0:T(8,128)(2,1)S(1)}, bf16[3,336,256]{2,1,0:T(8,128)(2,1)S(1)}, u32[]{:S(2)}, u32[]{:S(2)}) collective-permute-start(bf16[3,336,256]{2,1,0:T(8,128)(2,1)S(1)} %bitcast_select_fusion), channel_id=1, source_target_pairs={{0,8},{1,3},{2,10},{3,1},{4,12},{5,7},{6,14},{7,5},{8,0},{9,11},{1... | collective-permute-start | bytes 1548296 | tf_op jit(solution)/shard_map/ppermute | solution.py:22
  53.0 12.0 %copy-start.2 = (s32[32]{0:T(128)S(1)}, s32[32]{0:T(128)}, u32[]{:S(2)}) copy-start(s32[32]{0:T(128)} %rank_ref.1) | copy-start | bytes 388
  53.0 10.1 %collective-permute-start.12 = (bf16[2,336,384]{2,1,0:T(8,128)(2,1)S(1)}, bf16[2,336,384]{2,1,0:T(8,128)(2,1)S(1)}, u32[]{:S(2)}, u32[]{:S(2)}) collective-permute-start(bf16[2,336,384]{2,1,0:T(8,128)(2,1)S(1)} %broadcast_select_fusion), channel_id=1, source_target_pairs={{0,32},{1,97},{2,34},{3,99},{4,36},{5,101},{6,38},{7,103},{8,40},{... | collective-permute-start | bytes 1548296 | tf_op jit(solution)/shard_map/ppermute | solution.py:22
  63.0 2.0 %collective-permute-start.14 = (bf16[3,336,256]{2,1,0:T(8,128)(2,1)S(1)}, bf16[3,336,256]{2,1,0:T(8,128)(2,1)S(1)}, u32[]{:S(2)}, u32[]{:S(2)}) collective-permute-start(bf16[3,336,256]{2,1,0:T(8,128)(2,1)S(1)} %collective-permute-done.13.refs_12_), channel_id=1, source_target_pairs={{0,1},{1,0},{2,3},{3,2},{4,5},{5,4},{6,7},{7,6},{8,9},{9,8},{10,11... | collective-permute-start | bytes 1548296 | tf_op jit(solution)/shard_map/ppermute | solution.py:22
